TPU v7x, 256 devices: a whole 4x4x8 slice. The times are simulated.
256 devices in a mesh: row: 16 (over x, z_lo), col: 16 (over y, z_hi, core).
Axes of the slice: x: 4, y: 4, z: 8 (z_hi: 2, z_lo: 4; z = z_hi * 4 + z_lo), core: 2. Of those that a mesh axis runs over, the one named last changes fastest.
Arguments:
- query_proj: bfloat16 [128, 256, 768], P('row', 'col'), may hold values from -1 to 1
- key_proj: bfloat16 [128, 256, 768], P('row', 'col'), may hold values from -1 to 1
- value_proj: bfloat16 [128, 256, 768], P('row', 'col'), may hold values from -0.77734375 to 0.77734375
- grad_output: bfloat16 [128, 256, 768], P('row', 'col'), may hold values from -120 to 120
- log_totals: float32 [12, 256], P(None, 'col'), may hold values from 6 to 7.5
Outputs:
- grad_query: bfloat16 [128, 256, 768], P('row', 'col')
- grad_key: bfloat16 [128, 256, 768], P('row', 'col')
- grad_value: bfloat16 [128, 256, 768], P('row', 'col')
All inputs are finite; a program needn't handle non-finite values.
Results may differ from a plain program's by a relative error of at most 0.011.
Values may be sent and summed in bfloat16 or wider, within the bound.
A program may use at most 128 MiB of HBM per device.

v0:
```python
import jax
import jax.numpy as jnp
from jax import lax
from jax.sharding import PartitionSpec as P


def body(query_proj, key_proj, value_proj, grad_output, log_totals):
    seq_count, col_count, feat_count = query_proj.shape
    head_count = log_totals.shape[0]
    head_size = feat_count // head_count
    keys_all, values_all = (
        lax.all_gather(key_proj, "col", axis=1, tiled=True),
        lax.all_gather(value_proj, "col", axis=1, tiled=True),
    )
    total_cols = keys_all.shape[1]
    query_heads = query_proj.reshape(seq_count, col_count, head_count, head_size)
    output_heads = grad_output.reshape(seq_count, col_count, head_count, head_size)
    key_heads = keys_all.reshape(seq_count, total_cols, head_count, head_size)
    value_heads = values_all.reshape(seq_count, total_cols, head_count, head_size)
    logit_part = jnp.einsum(
        "rihe,rjhe->hij", query_heads, key_heads, preferred_element_type=jnp.float32
    )
    grad_part = jnp.einsum(
        "rihe,rjhe->hij", output_heads, value_heads, preferred_element_type=jnp.float32
    )
    logits, grad_probs = lax.psum((logit_part, grad_part), "row")
    probs = jnp.exp(logits - log_totals[:, :, None])
    delta = jnp.sum(probs * grad_probs, axis=2, keepdims=True)
    weights = probs.astype(jnp.bfloat16)
    grad_logits = (probs * (grad_probs - delta)).astype(jnp.bfloat16)
    grad_query = jnp.einsum(
        "hij,rjhe->rihe", grad_logits, key_heads, preferred_element_type=jnp.float32
    )
    grad_query = grad_query.reshape(seq_count, col_count, feat_count).astype(jnp.bfloat16)
    key_term = jnp.einsum(
        "hij,rihe->jrhe", grad_logits, query_heads, preferred_element_type=jnp.float32
    )
    value_term = jnp.einsum(
        "hij,rihe->jrhe", weights, output_heads, preferred_element_type=jnp.float32
    )
    stacked = jnp.stack((key_term, value_term), axis=1)
    reduced = lax.psum_scatter(
        stacked.reshape(col_count * lax.axis_size("col"), 2, seq_count, feat_count),
        "col",
        scatter_dimension=0,
        tiled=True,
    )
    grad_key = jnp.transpose(reduced[:, 0], (1, 0, 2)).astype(jnp.bfloat16)
    grad_value = jnp.transpose(reduced[:, 1], (1, 0, 2)).astype(jnp.bfloat16)
    return (grad_query, grad_key, grad_value)


def solution(mesh):
    in_specs = (
        P("row", "col", None),
        P("row", "col", None),
        P("row", "col", None),
        P("row", "col", None),
        P(None, "col"),
    )
    out_specs = (P("row", "col", None), P("row", "col", None), P("row", "col", None))
    return jax.shard_map(body, mesh=mesh, in_specs=in_specs, out_specs=out_specs, check_vma=False)
```

profile of v0, /device:TPU:1, one launch (start us, length us, event | category | flops | bytes accessed | tf_op | source)
XLA Modules:
  0.0 544.9 jit_solution(5121306593566366330)
XLA Ops:
  7.2 1.7 copy.26
  8.9 1.7 copy.30
  10.7 2.1 reshape.29
  12.8 2.1 reshape.31
  14.8 71.0 %all-gather.3.cloned.1.call-done = bf16[8,256,768]{2,0,1:T(8,128)(2,1)} async-done(((bf16[8,16,768]{2,0,1:T(8,128)(2,1)}), bf16[8,256,768]{2,0,1:T(8,128)(2,1)}) %all-gather.3.cloned.1.call-update) | async-done | bytes 3145744 | tf_op jit(solution)/shard_map/all_gather | solution.py:12
  85.8 3.8 copy.27
  89.6 2.7 fusion.15
  92.3 62.8 %all-gather.5.cloned.1.call-done = bf16[8,256,768]{2,0,1:T(8,128)(2,1)} async-done(((bf16[8,16,768]{2,0,1:T(8,128)(2,1)}), bf16[8,256,768]{2,0,1:T(8,128)(2,1)}) %all-gather.5.cloned.1.call-update) | async-done | bytes 3145744 | tf_op jit(solution)/shard_map/all_gather | solution.py:13
  155.1 5.1 copy.31
  160.2 3.4 fusion.18
  163.6 146.4 %all-reduce.3.cloned.1.call-done = (f32[12,16,256]{2,1,0:T(8,128)}, f32[12,16,256]{2,1,0:T(8,128)}) async-done(((f32[12,16,256]{2,1,0:T(8,128)}, f32[12,16,256]{2,1,0:T(8,128)}), (f32[12,16,256]{2,1,0:T(8,128)}, f32[12,16,256]{2,1,0:T(8,128)})) %all-reduce.3.cloned.1.call-update) | async-done | bytes 393232 | tf_op jit(solution)/shard_map/psum | solution.py:26
  310.1 4.7 convolution_bitcast_fusion
  314.8 4.1 convolution_bitcast_fusion.1
  318.9 6.4 %copy.37 = f32[256,8,12,64]{0,3,2,1:T(8,128)} copy(f32[256,8,12,64]{0,3,1,2:T(8,128)} %convolution_bitcast_fusion.1) | data formatting | bytes 12582912 | tf_op jit(solution)/shard_map/hij,rihe->jrhe/transpose | solution.py:35
  325.3 3.1 copy.39
  328.4 10.2 %pad_maximum_fusion = f32[256,2,8,768]{0,3,2,1:T(8,128)} fusion(f32[256,1,8,768]{0,3,2,1:T(8,128)} %bitcast.42, f32[256,1,8,768]{0,3,2,1:T(8,128)} %bitcast.41), kind=kLoop, calls=%fused_computation.1 | loop fusion | flops 3145728 | bytes 25165824 | tf_op jit(solution)/shard_map/stack | solution.py:41
  338.6 13.0 %copy.40 = f32[256,2,8,768]{3,2,1,0:T(8,128)} copy(f32[256,2,8,768]{0,3,2,1:T(8,128)} %pad_maximum_fusion) | data formatting | bytes 25165824 | tf_op jit(solution)/shard_map/stack | solution.py:41
  351.7 1.9 copy-done.1
  353.6 2.6 fusion.10
  356.5 1.0 convert_element_type.32
  357.5 178.3 %reduce-scatter.2.cloned.1.call-done = f32[16,2,8,768]{3,2,1,0:T(8,128)} async-done(((f32[256,2,8,768]{3,2,1,0:T(8,128)}), f32[16,2,8,768]{3,2,1,0:T(8,128)}) %reduce-scatter.2.cloned.1.call-update) | async-done | bytes 786448 | tf_op jit(solution)/shard_map/reduce_scatter | solution.py:42
  535.8 1.2 convert.4
  537.0 0.7 copy.42
  537.7 0.7 copy.41
  (28 shorter events, 0.6 us)
Async XLA Ops:
  7.2 78.6 %all-gather.3.cloned.1.call-start = ((), (), s32[]{:S(2)}) async-start(), calls=%async_computation.1 | async-start | bytes 3342336 | tf_op jit(solution)/shard_map/all_gather | solution.py:12
  8.9 146.2 %all-gather.5.cloned.1.call-start = ((), (), s32[]{:S(2)}) async-start(), calls=%async_computation.2 | async-start | bytes 3342336 | tf_op jit(solution)/shard_map/all_gather | solution.py:13
  10.6 299.4 %all-reduce.3.cloned.1.call-start = ((), (), s32[]{:S(2)}) async-start(), calls=%async_computation.4 | async-start | bytes 786432 | tf_op jit(solution)/shard_map/psum | solution.py:26
  89.6 70.5 %copy-start = (bf16[8,256,768]{1,2,0:T(8,128)(2,1)}, bf16[8,256,768]{1,2,0:T(8,128)(2,1)S(1)}, u32[]{:S(2)}) copy-start(bf16[8,256,768]{1,2,0:T(8,128)(2,1)S(1)} %copy.27) | copy-start | bytes 9437188
  160.1 149.9 %copy-start.6 = (f32[12,16]{1,0:T(8,128)S(1)}, f32[12,16]{1,0:T(8,128)}, u32[]{:S(2)}) copy-start(f32[12,16]{1,0:T(8,128)} %param.9) | copy-start | bytes 2308
  160.2 149.9 %copy-start.3 = (bf16[8,16,12,64]{3,2,1,0:T(8,128)(2,1)S(1)}, bf16[8,16,12,64]{3,2,1,0:T(8,128)(2,1)}, u32[]{:S(2)}) copy-start(bf16[8,16,12,64]{3,2,1,0:T(8,128)(2,1)} %reshape.31) | copy-start | bytes 589828
  163.5 372.2 %reduce-scatter.2.cloned.1.call-start = ((), (), s32[]{:S(2)}) async-start(), calls=%async_computation.3 | async-start | bytes 13369344 | tf_op jit(solution)/shard_map/reduce_scatter | solution.py:42
  310.0 4.8 copy-start.2
  310.0 4.8 copy-start.4
  310.0 4.8 copy-start.5
  314.8 10.5 %slice-start = ((s8[6291456]{0:T(1024)(128)(4,1)}), s8[2097152]{0:T(1024)(128)(4,1)S(1)}, s32[]{:S(2)}) async-start(s8[6291456]{0:T(1024)(128)(4,1)} %bitcast.39), calls=%async_computation.5 | async-start | bytes 4194304
  318.9 6.4 %slice-start.1 = ((s8[6291456]{0:T(1024)(128)(4,1)}), s8[4194304]{0:T(1024)(128)(4,1)S(1)}, s32[]{:S(2)}) async-start(s8[6291456]{0:T(1024)(128)(4,1)} %bitcast.39), calls=%async_computation.6 | async-start | bytes 8388608
  351.7 1.9 copy-start.1
Sparse Core Ops, SparseCore 0:
  11.3 74.4 all-gather.2
  89.0 66.0 all-gather.4
  163.7 146.3 all-reduce.2
  351.8 183.9 reduce-scatter.1
where the time goes:
time: 546 us; the launch traced here: 545 us
  waiting for transfers between devices  459 us (84%)
  local copies, waits for them, and re-layouts  43.5 us (8%)
  matrix products  17.5 us (3%)
  between operations  13.8 us (3%)
  other arithmetic  11.4 us (2%)
    reduce_scatter x1, waiting for transfers between devices, body(): lax.psum_scatter(stacked.reshape(col_count * lax.axis_size('col'), 2, seq...  178 us
    psum x1, waiting for transfers between devices, body(): logits, grad_probs = lax.psum((logit_part, grad_part), 'row')  146 us
    all_gather x1, waiting for transfers between devices, body(): lax.all_gather(key_proj, 'col', axis=1, tiled=True)  71 us
    all_gather x1, waiting for transfers between devices, body(): lax.all_gather(value_proj, 'col', axis=1, tiled=True)  62.8 us
    another operation x1, local copies, waits for them, and re-layouts, body(): stacked = jnp.stack((key_term, value_term), axis=1)  13 us
  transfers between devices with their start and end apart: 4, of which 4 were waited for; matrix products, arithmetic and copies ran while one was open for 3% of the time, Pallas kernels for 0%

commit v1 on v0

v1 whole, which is shorter than its diff:
```python
import jax
import jax.numpy as jnp
from jax import lax
from jax.experimental import pallas as pl
from jax.experimental.pallas import tpu as pltpu
from jax.sharding import PartitionSpec as P

MESH = pl.DeviceIdType.MESH
NX, NY, NZL, NZH, NC = 4, 4, 4, 2, 2
CH = 3
F32, BF16 = jnp.float32, jnp.bfloat16

ORDER = (
    ("in", 0), ("in", 1), ("in", 2),
    ("A", 0), ("B", 0), ("C", 0), ("A", 1), ("B", 1), ("D", 0), ("C", 1), ("E", 0),
    ("A", 2), ("k", 0), ("k", 1), ("k", 2), ("B", 2), ("F", 0), ("D", 1), ("C", 2), ("E", 1), ("F", 1), ("D", 2),
    ("G", 0), ("G", 1), ("E", 2), ("F", 2), ("G", 2), ("H", 0), ("H", 1), ("H", 2),
)


def swap_halves(low, high):
    lane = lax.broadcasted_iota(jnp.int32, low.shape, low.ndim - 1)
    first = jnp.concatenate([low[..., :64], high[..., :64]], axis=-1)
    second = jnp.concatenate([low[..., 64:], high[..., 64:]], axis=-1)
    del lane
    return first, second


def kernel(
    q_ref, k_ref, v_ref, g_ref, l_ref, dq_ref, dk_ref, dv_ref,
    st, rc, tt, c1, uu, x1, ww, z1, ag, oo, orr, lsend, lrecv,
    in_s, in_r, core_s, core_r, x_s, x_r, z_s, z_r, ga_s, ga_r, out_s, out_r, l_s, l_r,
):
    row, col = lax.axis_index("row"), lax.axis_index("col")
    x, zl = row // NZL, row % NZL
    y, zh, c = col // 4, (col // 2) % 2, col % 2
    here = y * 2 + c

    def dev(x, zl, y, zh, c):
        return (x * NZL + zl, (y * 2 + zh) * 2 + c)

    def send(src, dst, ssem, rsem, target):
        pltpu.make_async_remote_copy(
            src, dst, ssem, rsem, device_id=target, device_id_type=MESH
        ).start()

    def wait(ref, sem):
        pltpu.make_async_copy(ref, ref, sem).wait()

    def rot(value, step, count):
        return lax.rem(value + step, count)

    near = [(dy, dc) for dy in range(NY) for dc in range(NC)]

    l_to = dev(y, 2 * c + zl % 2, rot(x, 1, 4), zl // 2, zh)
    l_from = dev(rot(y, 3, 4), zh * 2 + zl % 2, x, c, zl // 2)

    barrier = pltpu.get_barrier_semaphore()
    peers = [dev(x, zl, rot(y, dy, 4), zh, rot(c, dc, 2)) for dy, dc in near[1:]]
    peers += [dev(x, zl, rot(y, dy, 4), 1 - zh, rot(c, dc, 2)) for dy, dc in near]
    peers += [dev(rot(x, d, 4), zl, y, zh, c) for d in range(1, 4)]
    peers += [dev(x, rot(zl, d, 4), y, zh, c) for d in range(1, 4)]
    peers += [dev(x, rot(zl, d, 4), y, 1 - zh, c) for d in range(1, 4)]
    peers += [l_from]
    for peer in peers:
        pl.semaphore_signal(barrier, inc=1, device_id=peer, device_id_type=MESH)

    def pack(ch):
        for a, ref in enumerate((q_ref, g_ref, k_ref, v_ref)):
            for yy in range(NY):
                head = yy * CH + ch
                tile = head // 2
                part = ref[:, :, tile * 128 : tile * 128 + 128].reshape(4, 2, 16, 128)
                block = swap_halves(part[:, 0], part[:, 1])[head % 2]
                for cc in range(NC):
                    st[ch, yy * 2 + cc, a] = block[2 * cc : 2 * cc + 2]

    sub = lax.broadcasted_iota(jnp.int32, (8, 16), 0) + 8 * (zl % 2)
    lane = lax.broadcasted_iota(jnp.int32, (8, 16), 1)
    for ch in range(CH):
        line = l_ref[pl.ds(rot(x, 1, 4) * CH + ch, 1), :]
        column = jnp.sum(jnp.where(sub == lane, line, 0.0), axis=1, keepdims=True)
        lsend[ch] = jnp.broadcast_to(column, (8, 128))

    pack(0)
    pl.semaphore_wait(barrier, len(peers))
    send(lsend, lrecv, l_s, l_r, l_to)

    def step_in(ch):
        if ch:
            pack(ch)
        for dy, dc in near:
            yy, cc = rot(y, dy, 4), rot(c, dc, 2)
            send(
                st.at[ch, yy * 2 + cc, pl.ds(0, 2)], rc.at[ch, zh, here, pl.ds(0, 2)],
                in_s.at[ch, 0], in_r.at[ch, 0], dev(x, zl, yy, 1 - zh, cc),
            )
        for dy, dc in near[1:]:
            yy, cc = rot(y, dy, 4), rot(c, dc, 2)
            send(
                st.at[ch, yy * 2 + cc], rc.at[ch, zh, here],
                in_s.at[ch, 1], in_r.at[ch, 1], dev(x, zl, yy, zh, cc),
            )
        pltpu.make_async_copy(st.at[ch, here], rc.at[ch, zh, here], in_r.at[ch, 1]).start()

    def step_k(ch):
        for dy, dc in near:
            yy, cc = rot(y, dy, 4), rot(c, dc, 2)
            send(
                st.at[ch, yy * 2 + cc, pl.ds(2, 1)], rc.at[ch, zh, here, pl.ds(2, 1)],
                in_s.at[ch, 2], in_r.at[ch, 2], dev(x, zl, yy, 1 - zh, cc),
            )

    def both(ch, a):
        return jnp.concatenate(
            [rc[ch, :, :, a, rp].reshape(256, 128) for rp in range(2)], axis=1
        )

    def half(ch, side, a):
        return jnp.concatenate(
            [rc[ch, side, :, a, rp].reshape(128, 128) for rp in range(2)], axis=1
        )

    def step_a(ch):
        wait(rc.at[ch, 1 - zh, :, pl.ds(0, 2)], in_r.at[ch, 0])
        wait(rc.at[ch, zh], in_r.at[ch, 1])
        for n, (left, right) in enumerate(((0, 2), (1, 3))):
            part = lax.dot_general(
                both(ch, left), half(ch, zh, right), (((1,), (1,)), ((), ())),
                preferred_element_type=F32,
            )
            tt[ch, :, n] = part.reshape(32, 8, 128)
        send(
            tt.at[ch, pl.ds((1 - c) * 16, 16)], c1.at[ch], core_s.at[ch], core_r.at[ch],
            dev(x, zl, y, zh, 1 - c),
        )

    def step_b(ch):
        wait(c1.at[ch], core_r.at[ch])
        total = tt[ch, pl.ds(c * 16, 16)] + c1[ch]
        uu[ch] = total.reshape(4, 4, 2, 8, 128)
        for d in (2, 1, 3):
            to = rot(x, d, 4)
            send(uu.at[ch, to], x1.at[ch, d - 1], x_s.at[ch], x_r.at[ch], dev(to, zl, y, zh, c))

    def step_c(ch):
        wait(x1.at[ch], x_r.at[ch])
        ww[ch] = (uu[ch, x] + x1[ch, 0]) + (x1[ch, 1] + x1[ch, 2])
        for d in range(4):
            to = rot(zl, d, 4)
            send(
                ww.at[ch, to], z1.at[ch, 3 + d], z_s.at[ch], z_r.at[ch], dev(x, to, y, 1 - zh, c)
            )
        for d in range(1, 4):
            to = rot(zl, d, 4)
            send(ww.at[ch, to], z1.at[ch, d - 1], z_s.at[ch], z_r.at[ch], dev(x, to, y, zh, c))

    def step_d(ch):
        if ch == 0:
            wait(lrecv, l_r)
        wait(z1.at[ch], z_r.at[ch])
        own = (ww[ch, zl] + z1[ch, 0]) + (z1[ch, 1] + z1[ch, 2])
        other = (z1[ch, 3] + z1[ch, 4]) + (z1[ch, 5] + z1[ch, 6])
        logs = lrecv[ch]
        p_own = jnp.exp(own[0] - logs)
        p_other = jnp.exp(other[0] - logs)
        delta = jnp.sum(p_own * own[1] + p_other * other[1], axis=1, keepdims=True)
        d_own = p_own * (own[1] - delta)
        d_other = p_other * (other[1] - delta)
        ag[ch, c, x, zl, 0] = jnp.concatenate([p_own, d_own], axis=0).astype(BF16)
        ag[ch, c, x, zl, 1] = jnp.concatenate([d_other, d_other], axis=0).astype(BF16)
        block = ag.at[ch, c, x, zl]
        for d in range(1, 4):
            send(
                block, block, ga_s.at[ch, 0, d - 1], ga_r.at[ch, 0, d - 1],
                dev(x, rot(zl, d, 4), y, zh, c),
            )

    def step_e(ch):
        for d in range(1, 4):
            wait(ag.at[ch, c, x, rot(zl, 4 - d, 4)], ga_r.at[ch, 0, d - 1])
        block = ag.at[ch, c, x]
        for d in (2, 1, 3):
            send(
                block, block, ga_s.at[ch, 1, d - 1], ga_r.at[ch, 1, d - 1],
                dev(rot(x, d, 4), zl, y, zh, c),
            )

    def step_f(ch):
        for d in range(1, 4):
            wait(ag.at[ch, c, rot(x, 4 - d, 4)], ga_r.at[ch, 1, d - 1])
        block = ag.at[ch, c]
        send(block, block, ga_s.at[ch, 2, 0], ga_r.at[ch, 2, 0], dev(x, zl, y, zh, 1 - c))

    def step_g(ch):
        wait(ag.at[ch, 1 - c], ga_r.at[ch, 2, 0])
        wait(rc.at[ch, 1 - zh, :, pl.ds(2, 1)], in_r.at[ch, 2])
        first = ag[ch, :, :, :, 0].reshape(32, 16, 128).astype(F32)
        weights = first[:, :8].reshape(256, 128).astype(BF16)
        slopes = first[:, 8:].reshape(256, 128).astype(BF16)
        mine = ag[ch, zh].reshape(16, 2, 16, 128).astype(F32)
        own = mine[:, 0, 8:].reshape(128, 128).astype(BF16)
        other = mine[:, 1, :8].reshape(128, 128).astype(BF16)
        down = (((0,), (0,)), ((), ()))
        across = (((1,), (0,)), ((), ()))
        dq = lax.dot_general(own, half(ch, zh, 2), across, preferred_element_type=F32)
        dq += lax.dot_general(other, half(ch, 1 - zh, 2), across, preferred_element_type=F32)
        dk = lax.dot_general(slopes, both(ch, 0), down, preferred_element_type=F32)
        dv = lax.dot_general(weights, both(ch, 1), down, preferred_element_type=F32)
        for a, value in enumerate((dq, dk, dv)):
            for rp in range(2):
                piece = value[:, rp * 128 : rp * 128 + 128].astype(BF16)
                oo[ch, :, a, rp] = piece.reshape(8, 16, 128)
        for dy, dc in near[1:]:
            yy, cc = rot(y, dy, 4), rot(c, dc, 2)
            send(
                oo.at[ch, yy * 2 + cc], orr.at[ch, here], out_s.at[ch], out_r.at[ch],
                dev(x, zl, yy, zh, cc),
            )
        pltpu.make_async_copy(oo.at[ch, here], orr.at[ch, here], out_r.at[ch]).start()

    def step_h(ch):
        wait(orr.at[ch], out_r.at[ch])

    steps = {
        "in": step_in, "k": step_k, "A": step_a, "B": step_b, "C": step_c, "D": step_d,
        "E": step_e, "F": step_f, "G": step_g, "H": step_h,
    }
    for name, ch in ORDER:
        steps[name](ch)

    for a, ref in enumerate((dq_ref, dk_ref, dv_ref)):
        for tile in range(6):
            pair = []
            for head in (2 * tile, 2 * tile + 1):
                yy, ch = head // CH, head % CH
                pair.append(orr[ch, pl.ds(yy * 2, 2), a].reshape(4, 16, 128))
            first, second = swap_halves(*pair)
            lanes = pl.ds(tile * 128, 128)
            for n in range(4):
                ref[2 * n, :, lanes] = first[n]
                ref[2 * n + 1, :, lanes] = second[n]

    wait(lsend, l_s)
    for ch in range(CH):
        wait(st.at[ch, :, pl.ds(0, 2)], in_s.at[ch, 0])
        wait(st.at[ch, pl.ds(0, 7)], in_s.at[ch, 1])
        wait(st.at[ch, :, pl.ds(2, 1)], in_s.at[ch, 2])
        wait(c1.at[ch], core_s.at[ch])
        wait(x1.at[ch], x_s.at[ch])
        wait(z1.at[ch], z_s.at[ch])
        for d in range(3):
            wait(ag.at[ch, c, x, zl], ga_s.at[ch, 0, d])
            wait(ag.at[ch, c, x], ga_s.at[ch, 1, d])
        wait(ag.at[ch, c], ga_s.at[ch, 2, 0])
        wait(oo.at[ch, pl.ds(0, 7)], out_s.at[ch])


def body(query_proj, key_proj, value_proj, grad_output, log_totals):
    dma = pltpu.SemaphoreType.DMA
    vmem = pl.BlockSpec(memory_space=pltpu.VMEM)
    return pl.pallas_call(
        kernel,
        out_shape=[jax.ShapeDtypeStruct(query_proj.shape, BF16)] * 3,
        in_specs=[vmem] * 5,
        out_specs=[vmem] * 3,
        scratch_shapes=[
            pltpu.VMEM((CH, 8, 4, 2, 16, 128), BF16),
            pltpu.VMEM((CH, 2, 8, 4, 2, 16, 128), BF16),
            pltpu.VMEM((CH, 32, 2, 8, 128), F32),
            pltpu.VMEM((CH, 16, 2, 8, 128), F32),
            pltpu.VMEM((CH, 4, 4, 2, 8, 128), F32),
            pltpu.VMEM((CH, 3, 4, 2, 8, 128), F32),
            pltpu.VMEM((CH, 4, 2, 8, 128), F32),
            pltpu.VMEM((CH, 7, 2, 8, 128), F32),
            pltpu.VMEM((CH, 2, 4, 4, 2, 16, 128), BF16),
            pltpu.VMEM((CH, 8, 3, 2, 16, 128), BF16),
            pltpu.VMEM((CH, 8, 3, 2, 16, 128), BF16),
            pltpu.VMEM((CH, 8, 128), F32),
            pltpu.VMEM((CH, 8, 128), F32),
            dma((CH, 3)), dma((CH, 3)),
            dma((CH,)), dma((CH,)),
            dma((CH,)), dma((CH,)),
            dma((CH,)), dma((CH,)),
            dma((CH, 3, 3)), dma((CH, 3, 3)),
            dma((CH,)), dma((CH,)),
            dma, dma,
        ],
        compiler_params=pltpu.CompilerParams(
            collective_id=0, has_side_effects=True, vmem_limit_bytes=40 * 2**20
        ),
        name="tied_row_backward",
    )(query_proj, key_proj, value_proj, grad_output, log_totals)


def solution(mesh):
    in_specs = (
        P("row", "col", None),
        P("row", "col", None),
        P("row", "col", None),
        P("row", "col", None),
        P(None, "col"),
    )
    out_specs = (P("row", "col", None), P("row", "col", None), P("row", "col", None))
    return jax.shard_map(body, mesh=mesh, in_specs=in_specs, out_specs=out_specs, check_vma=False)
```

time: 546 us -> 78.2 us (0.14)
  waiting for transfers between devices: 459 us -> 0 us
  Pallas kernels: 0 us -> 70.9 us
  local copies, waits for them, and re-layouts: 43.5 us -> 6.43 us
  matrix products: 17.5 us -> 0 us
  between operations: 13.8 us -> 0.65 us
  other arithmetic: 11.4 us -> 0 us
    reduce_scatter x1 -> x0, waiting for transfers between devices: 178 us -> none  [body(): lax.psum_scatter(stacked.reshape(col_count * lax.axis_size('col'), 2, seq...]
    psum x1 -> x0, waiting for transfers between devices: 146 us -> none  [body(): logits, grad_probs = lax.psum((logit_part, grad_part), 'row')]
    all_gather x2 -> x0, waiting for transfers between devices: 134 us -> none  [the longest x1 71 us: body(): lax.all_gather(key_proj, 'col', axis=1, tiled=True)]
    pallas_call x0 -> x1, Pallas kernels: none -> 70.9 us  [body(): pl.pallas_call(kernel, out_shape=[jax.ShapeDtypeStruct(query_proj.shape,...]
    dot_general x5 -> x0, matrix products: 17.5 us -> none  [the longest x1 4.74 us: body(): jnp.einsum('hij,rihe->jrhe', weights, output_heads, preferred_element_typ...]
    another operation x1 -> x0, local copies, waits for them, and re-layouts: 13 us -> none  [body(): stacked = jnp.stack((key_term, value_term), axis=1)]
    another operation x2 -> x0, other arithmetic: 11.4 us -> none  [the longest x1 10.2 us: body(): stacked = jnp.stack((key_term, value_term), axis=1)]
    transpose x2 -> x0, local copies, waits for them, and re-layouts: 9.5 us -> none  [the longest x1 6.39 us: body(): jnp.einsum('hij,rihe->jrhe', grad_logits, query_heads, preferred_element_...]
  transfers between devices with their start and end apart: 4 -> 0, of which waited for: 4 -> 0; matrix products, arithmetic and copies ran while one was open for 3% -> 0% of each run, Pallas kernels for 0% -> 0%
where the time goes in v1:
time: 78.2 us; the launch traced here: 78 us
  Pallas kernels  70.9 us (91%)
  local copies, waits for them, and re-layouts  6.43 us (8%)
    pallas_call x1, Pallas kernels, body(): pl.pallas_call(kernel, out_shape=[jax.ShapeDtypeStruct(query_proj.shape,...  70.9 us
    unnamed x13, local copies, waits for them, and re-layouts  6.43 us

profile of v1, /device:TPU:1, one launch (start us, length us, event | category | flops | bytes accessed | tf_op | source)
XLA Modules:
  0.0 78.0 jit_solution(10791066483098058374)
XLA Ops:
  0.6 0.0 copy-start
  0.6 0.9 %copy-done = bf16[8,16,768]{2,1,0:T(8,128)(2,1)S(1)} copy-done((bf16[8,16,768]{2,1,0:T(8,128)(2,1)S(1)}, bf16[8,16,768]{2,1,0:T(8,128)(2,1)}, u32[]{:S(2)}) %copy-start) | copy-done | bytes 196632
  1.6 0.0 copy-start.1
  1.6 0.9 %copy-done.1 = bf16[8,16,768]{2,1,0:T(8,128)(2,1)S(1)} copy-done((bf16[8,16,768]{2,1,0:T(8,128)(2,1)S(1)}, bf16[8,16,768]{2,1,0:T(8,128)(2,1)}, u32[]{:S(2)}) %copy-start.1) | copy-done | bytes 196632
  2.5 0.0 copy-start.2
  2.5 0.9 %copy-done.2 = bf16[8,16,768]{2,1,0:T(8,128)(2,1)S(1)} copy-done((bf16[8,16,768]{2,1,0:T(8,128)(2,1)S(1)}, bf16[8,16,768]{2,1,0:T(8,128)(2,1)}, u32[]{:S(2)}) %copy-start.2) | copy-done | bytes 196632
  3.4 0.0 copy-start.3
  3.4 0.9 %copy-done.3 = bf16[8,16,768]{2,1,0:T(8,128)(2,1)S(1)} copy-done((bf16[8,16,768]{2,1,0:T(8,128)(2,1)S(1)}, bf16[8,16,768]{2,1,0:T(8,128)(2,1)}, u32[]{:S(2)}) %copy-start.3) | copy-done | bytes 196632
  4.3 0.0 copy-start.4
  4.3 0.7 copy-done.4
  5.0 70.9 %tied_row_backward.1 = (bf16[8,16,768]{2,1,0:T(8,128)(2,1)S(1)}, bf16[8,16,768]{2,1,0:T(8,128)(2,1)S(1)}, bf16[8,16,768]{2,1,0:T(8,128)(2,1)S(1)}) custom-call(bf16[8,16,768]{2,1,0:T(8,128)(2,1)S(1)} %copy-done, bf16[8,16,768]{2,1,0:T(8,128)(2,1)S(1)} %copy-done.1, bf16[8,16,768]{2,1,0:T(8,128)(2,1)S(1)} %copy-done.2, bf16[8,16,768]{2,1,0:T(8,128)(2,1)S(1)} %copy-done.3, ...), custom_call_target="tpu_custom_call" | custom-call | tf_op jit(solution)/shard_map/tied_row_backward/pallas_call | solution.py:262
  76.0 0.7 copy.11
  76.6 0.7 copy.12
  77.3 0.7 copy.13
Async XLA Ops:
  0.6 0.9 %copy-start = (bf16[8,16,768]{2,1,0:T(8,128)(2,1)S(1)}, bf16[8,16,768]{2,1,0:T(8,128)(2,1)}, u32[]{:S(2)}) copy-start(bf16[8,16,768]{2,1,0:T(8,128)(2,1)} %q_ref.1) | copy-start | bytes 589828
  1.6 0.9 %copy-start.1 = (bf16[8,16,768]{2,1,0:T(8,128)(2,1)S(1)}, bf16[8,16,768]{2,1,0:T(8,128)(2,1)}, u32[]{:S(2)}) copy-start(bf16[8,16,768]{2,1,0:T(8,128)(2,1)} %k_ref.1) | copy-start | bytes 589828
  2.5 0.9 %copy-start.2 = (bf16[8,16,768]{2,1,0:T(8,128)(2,1)S(1)}, bf16[8,16,768]{2,1,0:T(8,128)(2,1)}, u32[]{:S(2)}) copy-start(bf16[8,16,768]{2,1,0:T(8,128)(2,1)} %v_ref.1) | copy-start | bytes 589828
  3.4 0.9 %copy-start.3 = (bf16[8,16,768]{2,1,0:T(8,128)(2,1)S(1)}, bf16[8,16,768]{2,1,0:T(8,128)(2,1)}, u32[]{:S(2)}) copy-start(bf16[8,16,768]{2,1,0:T(8,128)(2,1)} %g_ref.1) | copy-start | bytes 589828
  4.3 0.7 copy-start.4

commit v2 on v1

v2 whole, which is shorter than its diff:
```python
import jax
import jax.numpy as jnp
from jax import lax
from jax.experimental import pallas as pl
from jax.experimental.pallas import tpu as pltpu
from jax.sharding import PartitionSpec as P

MESH = pl.DeviceIdType.MESH
NY, NC = 4, 2
CH = 3
F32, BF16 = jnp.float32, jnp.bfloat16
Q, K, G, V = 0, 1, 2, 3
S, D = 0, 1

ORDER = (
    "I0", "L0", "I1", "I2", "J0", "J1", "J2", "As0", "Bs0", "As1", "Bs1", "As2", "Bs2", "Cs0",
    "Cs1", "Cs2", "K0", "K1", "Ad0", "Bd0", "Ad1", "Bd1", "Cd0", "Ad2", "Bd2", "Cd1", "Cd2", "Ds0",
    "Ds1", "Ds2", "Dp0", "Dd0", "Dd1", "Dd2", "K2", "Ep0", "Ed0", "Ed1", "Ed2", "Fp0", "Fd0", "Fd1",
    "Fd2", "Gp0", "Gp1", "Gp2", "Gd0", "Gd1", "Gd2", "Hp0", "Hd0",
)


def swap_halves(low, high):
    first = jnp.concatenate([low[..., :64], high[..., :64]], axis=-1)
    second = jnp.concatenate([low[..., 64:], high[..., 64:]], axis=-1)
    return first, second


def kernel(
    q_hbm, k_hbm, v_hbm, g_hbm, l_hbm, dq_hbm, dk_hbm, dv_hbm,
    q_ref, k_ref, v_ref, g_ref, l_ref, dq_ref, dk_ref, dv_ref, load_s, store_s,
    st, rc, tt, c1, uu, x1, ww, z1, pp, agp, psend, agd, dsend, oo, orr, lsend, lrecv,
    in_s, in_r, core_s, core_r, x_s, x_r, z_s, z_r, gp_s, gp_r, gd_s, gd_r, out_s, out_r, l_s, l_r,
):
    row, col = lax.axis_index("row"), lax.axis_index("col")
    x, zl = row // 4, row % 4
    y, zh, c = col // 4, (col // 2) % 2, col % 2
    here = y * 2 + c

    def dev(x, zl, y, zh, c):
        return (x * 4 + zl, (y * 2 + zh) * 2 + c)

    def send(src, dst, ssem, rsem, target):
        pltpu.make_async_remote_copy(
            src, dst, ssem, rsem, device_id=target, device_id_type=MESH
        ).start()

    def wait(ref, sem):
        pltpu.make_async_copy(ref, ref, sem).wait()

    def rot(value, step, count):
        return lax.rem(value + step, count)

    loads = [
        pltpu.make_async_copy(src, dst, load_s.at[n])
        for n, (src, dst) in enumerate((
            (q_hbm, q_ref), (k_hbm, k_ref), (g_hbm, g_ref), (v_hbm, v_ref), (l_hbm, l_ref)
        ))
    ]
    for load in loads:
        load.start()

    near = [(dy, dc) for dy in range(NY) for dc in range(NC)]
    core_peer = dev(x, zl, y, zh, 1 - c)

    def along(step):
        z = rot(zh * 4 + zl, step, 8)
        return z % 4, z // 4

    l_to = dev(y, 2 * c + zl % 2, rot(x, 1, 4), zl // 2, zh)
    l_from = dev(rot(y, 3, 4), zh * 2 + zl % 2, x, c, zl // 2)

    barrier = pltpu.get_barrier_semaphore()
    peers = [dev(x, zl, rot(y, dy, 4), zh, rot(c, dc, 2)) for dy, dc in near[1:]]
    peers += [dev(x, zl, rot(y, dy, 4), 1 - zh, rot(c, dc, 2)) for dy, dc in near]
    peers += [dev(rot(x, d, 4), zl, y, zh, c) for d in range(1, 4)]
    peers += [dev(x, rot(zl, d, 4), y, zh, c) for d in range(1, 4)]
    peers += [dev(x, rot(zl, d, 4), y, 1 - zh, c) for d in range(1, 4)]
    peers += [l_from]
    for peer in peers:
        pl.semaphore_signal(barrier, inc=1, device_id=peer, device_id_type=MESH)

    def pack(ch, arrays):
        for a, ref in arrays:
            for yy in range(NY):
                head = yy * CH + ch
                tile = head // 2
                part = ref[:, :, tile * 128 : tile * 128 + 128].reshape(4, 2, 16, 128)
                block = swap_halves(part[:, 0], part[:, 1])[head % 2]
                for cc in range(NC):
                    st[ch, yy * 2 + cc, a] = block[2 * cc : 2 * cc + 2]

    loads[0].wait()
    loads[1].wait()
    pack(0, ((Q, q_ref), (K, k_ref)))
    pl.semaphore_wait(barrier, len(peers))

    def cross(ch, a, n):
        for dy, dc in near:
            yy, cc = rot(y, dy, 4), rot(c, dc, 2)
            send(
                st.at[ch, yy * 2 + cc, pl.ds(a, 1)], rc.at[ch, zh, here, pl.ds(a, 1)],
                in_s.at[ch, n], in_r.at[ch, n], dev(x, zl, yy, 1 - zh, cc),
            )

    def within(ch, a, n):
        for dy, dc in near[1:]:
            yy, cc = rot(y, dy, 4), rot(c, dc, 2)
            send(
                st.at[ch, yy * 2 + cc, pl.ds(a, 2)], rc.at[ch, zh, here, pl.ds(a, 2)],
                in_s.at[ch, n], in_r.at[ch, n], dev(x, zl, yy, zh, cc),
            )
        pltpu.make_async_copy(
            st.at[ch, here, pl.ds(a, 2)], rc.at[ch, zh, here, pl.ds(a, 2)], in_r.at[ch, n]
        ).start()

    def step_i(ch):
        if ch:
            pack(ch, ((Q, q_ref), (K, k_ref)))
        cross(ch, Q, 0)
        within(ch, Q, 1)

    def step_j(ch):
        if ch == 0:
            loads[2].wait()
            loads[3].wait()
        pack(ch, ((G, g_ref), (V, v_ref)))
        cross(ch, G, 2)
        within(ch, G, 3)

    def step_l(ch):
        loads[4].wait()
        sub = lax.broadcasted_iota(jnp.int32, (8, 16), 0) + 8 * (zl % 2)
        lane = lax.broadcasted_iota(jnp.int32, (8, 16), 1)
        for n in range(CH):
            line = l_ref[pl.ds(rot(x, 1, 4) * CH + n, 1), :]
            column = jnp.sum(jnp.where(sub == lane, line, 0.0), axis=1, keepdims=True)
            lsend[n] = jnp.broadcast_to(column, (8, 128))
        send(lsend, lrecv, l_s, l_r, l_to)

    def step_k(ch):
        cross(ch, K, 4)

    def both(ch, a):
        return jnp.concatenate(
            [rc[ch, :, :, a, rp].reshape(256, 128) for rp in range(2)], axis=1
        )

    def half(ch, side, a):
        return jnp.concatenate(
            [rc[ch, side, :, a, rp].reshape(128, 128) for rp in range(2)], axis=1
        )

    def step_a(ch, n):
        a = (Q, G)[n]
        wait(rc.at[ch, zh, :, pl.ds(a, 2)], in_r.at[ch, 2 * n + 1])
        wait(rc.at[ch, 1 - zh, :, pl.ds(a, 1)], in_r.at[ch, 2 * n])
        part = lax.dot_general(
            both(ch, a), half(ch, zh, a + 1), (((1,), (1,)), ((), ())),
            preferred_element_type=F32,
        )
        tt[ch, n] = part.reshape(32, 8, 128)
        send(
            tt.at[ch, n, pl.ds((1 - c) * 16, 16)], c1.at[ch, n],
            core_s.at[ch, n], core_r.at[ch, n], core_peer,
        )

    def step_b(ch, n):
        wait(c1.at[ch, n], core_r.at[ch, n])
        total = tt[ch, n, pl.ds(c * 16, 16)] + c1[ch, n]
        uu[ch, n] = total.reshape(4, 4, 8, 128)
        for d in (2, 1, 3):
            to = rot(x, d, 4)
            send(
                uu.at[ch, n, to], x1.at[ch, n, d - 1], x_s.at[ch, n], x_r.at[ch, n],
                dev(to, zl, y, zh, c),
            )

    def step_c(ch, n):
        wait(x1.at[ch, n], x_r.at[ch, n])
        ww[ch, n] = (uu[ch, n, x] + x1[ch, n, 0]) + (x1[ch, n, 1] + x1[ch, n, 2])
        for d in range(4):
            to = rot(zl, d, 4)
            send(
                ww.at[ch, n, to], z1.at[ch, n, 3 + d], z_s.at[ch, n], z_r.at[ch, n],
                dev(x, to, y, 1 - zh, c),
            )
        for d in range(1, 4):
            to = rot(zl, d, 4)
            send(
                ww.at[ch, n, to], z1.at[ch, n, d - 1], z_s.at[ch, n], z_r.at[ch, n],
                dev(x, to, y, zh, c),
            )

    def sums(ch, n):
        wait(z1.at[ch, n], z_r.at[ch, n])
        own = (ww[ch, n, zl] + z1[ch, n, 0]) + (z1[ch, n, 1] + z1[ch, n, 2])
        other = (z1[ch, n, 3] + z1[ch, n, 4]) + (z1[ch, n, 5] + z1[ch, n, 6])
        return own, other

    def step_p(ch):
        if ch == 0:
            wait(lrecv, l_r)
        own, other = sums(ch, S)
        pp[ch, 0] = jnp.exp(own - lrecv[ch])
        pp[ch, 1] = jnp.exp(other - lrecv[ch])

    def gather_z(mine, swapped, dst, ssem, rsem):
        for n, step in enumerate((2, 1, 7)):
            to_zl, to_zh = along(step)
            target = dev(x, to_zl, y, to_zh, c)

            @pl.when(to_zh == zh)
            def _():
                send(mine, dst, ssem.at[n], rsem.at[n], target)

            @pl.when(to_zh != zh)
            def _():
                send(swapped, dst, ssem.at[n], rsem.at[n], target)

    def gather_x(whole, got, ssem, rsem, z_recv):
        for n, step in enumerate((6, 7, 1)):
            wait(got(c, x, along(step)[0]), z_recv.at[n])
        block = whole.at[c, x]
        for n, d in enumerate((2, 1, 3)):
            send(block, block, ssem.at[n], rsem.at[n], dev(rot(x, d, 4), zl, y, zh, c))

    def gather_core(whole, ssem, rsem, x_recv):
        for n, d in enumerate((2, 3, 1)):
            wait(whole.at[c, rot(x, d, 4)], x_recv.at[n])
        send(whole.at[c], whole.at[c], ssem, rsem, core_peer)

    def step_dp(ch):
        for side, place in ((0, agp.at[c, x, zl]), (1, psend)):
            place[0] = jnp.concatenate([pp[0, side], pp[1, side]], axis=0).astype(BF16)
            place[1] = jnp.concatenate([pp[2, side], pp[2, side]], axis=0).astype(BF16)
        gather_z(agp.at[c, x, zl], psend, agp.at[c, x, zl], gp_s.at[0], gp_r.at[0])

    def step_ep(ch):
        gather_x(agp, lambda *at: agp.at[at], gp_s.at[1], gp_r.at[1], gp_r.at[0])

    def step_fp(ch):
        gather_core(agp, gp_s.at[2, 0], gp_r.at[2, 0], gp_r.at[1])

    def step_dd(ch):
        own, other = sums(ch, D)
        p_own, p_other = pp[ch, 0], pp[ch, 1]
        delta = jnp.sum(p_own * own + p_other * other, axis=1, keepdims=True)
        d_own = p_own * (own - delta)
        d_other = p_other * (other - delta)
        place = agd.at[ch, c, x, zl]
        place[...] = jnp.concatenate([d_own, d_other], axis=0).astype(BF16)
        dsend[ch] = jnp.concatenate([d_other, d_own], axis=0).astype(BF16)
        gather_z(place, dsend.at[ch], place, gd_s.at[ch, 0], gd_r.at[ch, 0])

    def step_ed(ch):
        gather_x(
            agd.at[ch], lambda *at: agd.at[(ch, *at)], gd_s.at[ch, 1], gd_r.at[ch, 1], gd_r.at[ch, 0]
        )

    def step_fd(ch):
        gather_core(agd.at[ch], gd_s.at[ch, 2, 0], gd_r.at[ch, 2, 0], gd_r.at[ch, 1])

    down = (((0,), (0,)), ((), ()))
    across = (((1,), (0,)), ((), ()))

    def put(ch, a, value):
        for rp in range(2):
            piece = value[:, rp * 128 : rp * 128 + 128].astype(BF16)
            oo[ch, :, a, rp] = piece.reshape(8, 16, 128)

    def give(ch, part, n):
        for dy, dc in near[1:]:
            yy, cc = rot(y, dy, 4), rot(c, dc, 2)
            send(
                oo.at[ch, yy * 2 + cc, part], orr.at[ch, here, part],
                out_s.at[ch, n], out_r.at[ch, n], dev(x, zl, yy, zh, cc),
            )
        pltpu.make_async_copy(
            oo.at[ch, here, part], orr.at[ch, here, part], out_r.at[ch, n]
        ).start()

    def step_gp(ch):
        if ch == 0:
            wait(agp.at[1 - c], gp_r.at[2, 0])
        tile = agp[:, :, :, ch // 2].reshape(32, 16, 128).astype(F32)
        start = 8 * (ch % 2)
        weights = tile[:, start : start + 8].reshape(256, 128).astype(BF16)
        put(ch, 2, lax.dot_general(weights, both(ch, G), down, preferred_element_type=F32))
        give(ch, pl.ds(2, 1), 0)

    def step_gd(ch):
        wait(agd.at[ch, 1 - c], gd_r.at[ch, 2, 0])
        tile = agd[ch].reshape(32, 16, 128).astype(F32)
        slopes = tile[:, :8].reshape(256, 128).astype(BF16)
        put(ch, 1, lax.dot_general(slopes, both(ch, Q), down, preferred_element_type=F32))
        wait(rc.at[ch, 1 - zh, :, pl.ds(K, 1)], in_r.at[ch, 4])
        mine = agd[ch, zh].reshape(16, 16, 128).astype(F32)
        own = mine[:, :8].reshape(128, 128).astype(BF16)
        other = mine[:, 8:].reshape(128, 128).astype(BF16)
        dq = lax.dot_general(own, half(ch, zh, K), across, preferred_element_type=F32)
        dq += lax.dot_general(other, half(ch, 1 - zh, K), across, preferred_element_type=F32)
        put(ch, 0, dq)
        give(ch, pl.ds(0, 2), 1)

    def unpack(a, ref, hbm):
        for tile in range(6):
            pair = []
            for head in (2 * tile, 2 * tile + 1):
                yy, ch = head // CH, head % CH
                pair.append(orr[ch, pl.ds(yy * 2, 2), a].reshape(4, 16, 128))
            first, second = swap_halves(*pair)
            lanes = pl.ds(tile * 128, 128)
            for n in range(4):
                ref[2 * n, :, lanes] = first[n]
                ref[2 * n + 1, :, lanes] = second[n]
        pltpu.make_async_copy(ref, hbm, store_s.at[a]).start()

    def step_hp(ch):
        for n in range(CH):
            wait(orr.at[n, :, pl.ds(2, 1)], out_r.at[n, 0])
        unpack(2, dv_ref, dv_hbm)

    def step_hd(ch):
        for n in range(CH):
            wait(orr.at[n, :, pl.ds(0, 2)], out_r.at[n, 1])
        unpack(1, dk_ref, dk_hbm)
        unpack(0, dq_ref, dq_hbm)

    steps = {
        "I": step_i, "J": step_j, "K": step_k, "L": step_l,
        "As": lambda ch: step_a(ch, S), "Ad": lambda ch: step_a(ch, D),
        "Bs": lambda ch: step_b(ch, S), "Bd": lambda ch: step_b(ch, D),
        "Cs": lambda ch: step_c(ch, S), "Cd": lambda ch: step_c(ch, D),
        "Ds": step_p, "Dp": step_dp, "Ep": step_ep, "Fp": step_fp, "Gp": step_gp, "Hp": step_hp,
        "Dd": step_dd, "Ed": step_ed, "Fd": step_fd, "Gd": step_gd, "Hd": step_hd,
    }
    for name in ORDER:
        steps[name[:-1]](int(name[-1]))

    wait(lsend, l_s)
    wait(agp.at[c], gp_s.at[2, 0])
    for n in range(3):
        wait(agp.at[c, x, zl], gp_s.at[0, n])
        wait(agp.at[c, x], gp_s.at[1, n])
    for ch in range(CH):
        for a, n in ((Q, 0), (G, 2), (K, 4)):
            wait(st.at[ch, :, pl.ds(a, 1)], in_s.at[ch, n])
        for a, n in ((Q, 1), (G, 3)):
            wait(st.at[ch, pl.ds(0, 7), pl.ds(a, 2)], in_s.at[ch, n])
        for n in range(2):
            wait(c1.at[ch, n], core_s.at[ch, n])
            wait(x1.at[ch, n], x_s.at[ch, n])
            wait(z1.at[ch, n], z_s.at[ch, n])
        for n in range(3):
            wait(agd.at[ch, c, x, zl], gd_s.at[ch, 0, n])
            wait(agd.at[ch, c, x], gd_s.at[ch, 1, n])
        wait(agd.at[ch, c], gd_s.at[ch, 2, 0])
        wait(oo.at[ch, pl.ds(0, 7), pl.ds(2, 1)], out_s.at[ch, 0])
        wait(oo.at[ch, pl.ds(0, 7), pl.ds(0, 2)], out_s.at[ch, 1])
    for a, (ref, hbm) in enumerate(((dq_ref, dq_hbm), (dk_ref, dk_hbm), (dv_ref, dv_hbm))):
        pltpu.make_async_copy(ref, hbm, store_s.at[a]).wait()


def body(query_proj, key_proj, value_proj, grad_output, log_totals):
    dma = pltpu.SemaphoreType.DMA
    anywhere = pl.BlockSpec(memory_space=pl.ANY)
    return pl.pallas_call(
        kernel,
        out_shape=[jax.ShapeDtypeStruct(query_proj.shape, BF16)] * 3,
        in_specs=[anywhere] * 5,
        out_specs=[anywhere] * 3,
        scratch_shapes=[
            *[pltpu.VMEM(query_proj.shape, BF16)] * 4,
            pltpu.VMEM(log_totals.shape, F32),
            *[pltpu.VMEM(query_proj.shape, BF16)] * 3,
            dma((5,)), dma((3,)),
            pltpu.VMEM((CH, 8, 4, 2, 16, 128), BF16),
            pltpu.VMEM((CH, 2, 8, 4, 2, 16, 128), BF16),
            pltpu.VMEM((CH, 2, 32, 8, 128), F32),
            pltpu.VMEM((CH, 2, 16, 8, 128), F32),
            pltpu.VMEM((CH, 2, 4, 4, 8, 128), F32),
            pltpu.VMEM((CH, 2, 3, 4, 8, 128), F32),
            pltpu.VMEM((CH, 2, 4, 8, 128), F32),
            pltpu.VMEM((CH, 2, 7, 8, 128), F32),
            pltpu.VMEM((CH, 2, 8, 128), F32),
            pltpu.VMEM((2, 4, 4, 2, 16, 128), BF16),
            pltpu.VMEM((2, 16, 128), BF16),
            pltpu.VMEM((CH, 2, 4, 4, 16, 128), BF16),
            pltpu.VMEM((CH, 16, 128), BF16),
            pltpu.VMEM((CH, 8, 3, 2, 16, 128), BF16),
            pltpu.VMEM((CH, 8, 3, 2, 16, 128), BF16),
            pltpu.VMEM((CH, 8, 128), F32),
            pltpu.VMEM((CH, 8, 128), F32),
            dma((CH, 5)), dma((CH, 5)),
            dma((CH, 2)), dma((CH, 2)),
            dma((CH, 2)), dma((CH, 2)),
            dma((CH, 2)), dma((CH, 2)),
            dma((3, 3)), dma((3, 3)),
            dma((CH, 3, 3)), dma((CH, 3, 3)),
            dma((CH, 2)), dma((CH, 2)),
            dma, dma,
        ],
        compiler_params=pltpu.CompilerParams(
            collective_id=0, has_side_effects=True, vmem_limit_bytes=60 * 2**20
        ),
        name="tied_row_backward",
    )(query_proj, key_proj, value_proj, grad_output, log_totals)


def solution(mesh):
    in_specs = (
        P("row", "col", None),
        P("row", "col", None),
        P("row", "col", None),
        P("row", "col", None),
        P(None, "col"),
    )
    out_specs = (P("row", "col", None), P("row", "col", None), P("row", "col", None))
    return jax.shard_map(body, mesh=mesh, in_specs=in_specs, out_specs=out_specs, check_vma=False)
```

time: 78.2 us -> 68.9 us (0.88)
  Pallas kernels: 70.9 us -> 64.7 us
  local copies, waits for them, and re-layouts: 6.43 us -> 3.33 us
    pallas_call x1, Pallas kernels: 70.9 us -> 64.7 us  [body(): pl.pallas_call(kernel, out_shape=[jax.ShapeDtypeStruct(query_proj.shape,...]
    unnamed x13 -> x7, local copies, waits for them, and re-layouts: 6.43 us -> 3.33 us
where the time goes in v2:
time: 68.9 us; the launch traced here: 68.7 us
  Pallas kernels  64.7 us (94%)
  local copies, waits for them, and re-layouts  3.33 us (5%)
    pallas_call x1, Pallas kernels, body(): pl.pallas_call(kernel, out_shape=[jax.ShapeDtypeStruct(query_proj.shape,...  64.7 us
    unnamed x7, local copies, waits for them, and re-layouts  3.33 us

profile of v2, /device:TPU:1, one launch (start us, length us, event | category | flops | bytes accessed | tf_op | source)
XLA Modules:
  0.0 68.7 jit_solution(14748637901226519661)
XLA Ops:
  0.6 64.7 %tied_row_backward.1 = (bf16[8,16,768]{2,1,0:T(8,128)(2,1)}, bf16[8,16,768]{2,1,0:T(8,128)(2,1)}, bf16[8,16,768]{2,1,0:T(8,128)(2,1)}) custom-call(bf16[8,16,768]{2,1,0:T(8,128)(2,1)} %q_hbm.1, bf16[8,16,768]{2,1,0:T(8,128)(2,1)} %k_hbm.1, bf16[8,16,768]{2,1,0:T(8,128)(2,1)} %v_hbm.1, bf16[8,16,768]{2,1,0:T(8,128)(2,1)} %g_hbm.1, f32[12,16]{1,0:T(8,128)} %l_hbm.1), custom_call_target="tpu_custom_call" | custom-call | tf_op jit(solution)/shard_map/tied_row_backward/pallas_call | solution.py:368
  65.4 0.0 copy-start.1
  65.4 1.7 %copy.11 = bf16[8,16,768]{2,1,0:T(8,128)(2,1)} copy(bf16[8,16,768]{2,1,0:T(8,128)(2,1)} %get-tuple-element.6) | data formatting | bytes 393216
  67.0 0.0 copy-done.1
  67.0 0.0 copy-start
  67.0 0.7 copy.12
  67.7 0.3 copy-done
  68.0 0.7 copy.13
Async XLA Ops:
  65.4 1.7 %copy-start.1 = (bf16[8,16,768]{2,1,0:T(8,128)(2,1)S(1)}, bf16[8,16,768]{2,1,0:T(8,128)(2,1)}, u32[]{:S(2)}) copy-start(bf16[8,16,768]{2,1,0:T(8,128)(2,1)} %get-tuple-element.7) | copy-start | bytes 589828
  67.0 1.0 %copy-start = (bf16[8,16,768]{2,1,0:T(8,128)(2,1)S(1)}, bf16[8,16,768]{2,1,0:T(8,128)(2,1)}, u32[]{:S(2)}) copy-start(bf16[8,16,768]{2,1,0:T(8,128)(2,1)} %get-tuple-element.8) | copy-start | bytes 589828

commit v3 on v2

--- a/solution.py
+++ b/solution.py
@@ -14,9 +14,9 @@
 
 ORDER = (
     "I0", "L0", "I1", "I2", "J0", "J1", "J2", "As0", "Bs0", "As1", "Bs1", "As2", "Bs2", "Cs0",
-    "Cs1", "Cs2", "K0", "K1", "Ad0", "Bd0", "Ad1", "Bd1", "Cd0", "Ad2", "Bd2", "Cd1", "Cd2", "Ds0",
-    "Ds1", "Ds2", "Dp0", "Dd0", "Dd1", "Dd2", "K2", "Ep0", "Ed0", "Ed1", "Ed2", "Fp0", "Fd0", "Fd1",
-    "Fd2", "Gp0", "Gp1", "Gp2", "Gd0", "Gd1", "Gd2", "Hp0", "Hd0",
+    "Cs1", "Cs2", "K0", "K1", "Ad0", "Ad1", "Cd0", "Ad2", "Cd1", "Cd2", "Ds0", "Ds1", "Ds2", "Dp0",
+    "Dd0", "Dd1", "Dd2", "K2", "Ep0", "Ed0", "Ed1", "Ed2", "Fp0", "Fd0", "Fd1", "Fd2", "Gp0", "Gp1",
+    "Gp2", "Gd0", "Gd1", "Gd2", "Hp0", "Hd0",
 )
 
 
@@ -27,9 +27,9 @@
 
 
 def kernel(
-    q_hbm, k_hbm, v_hbm, g_hbm, l_hbm, dq_hbm, dk_hbm, dv_hbm,
-    q_ref, k_ref, v_ref, g_ref, l_ref, dq_ref, dk_ref, dv_ref, load_s, store_s,
-    st, rc, tt, c1, uu, x1, ww, z1, pp, agp, psend, agd, dsend, oo, orr, lsend, lrecv,
+    q_hbm, k_hbm, v_hbm, g_hbm, l_hbm, orr,
+    q_ref, k_ref, v_ref, g_ref, l_ref, load_s,
+    st, rc, tt, tb, xb, c1, uu, x1, ww, z1, pp, agp, psend, agd, dsend, oo, lsend, lrecv,
     in_s, in_r, core_s, core_r, x_s, x_r, z_s, z_r, gp_s, gp_r, gd_s, gd_r, out_s, out_r, l_s, l_r,
 ):
     row, col = lax.axis_index("row"), lax.axis_index("col")
@@ -60,6 +60,7 @@
     for load in loads:
         load.start()
 
+    others = [(dx, dc) for dx in (2, 1, 3, 0) for dc in (1, 0) if dx or dc]
     near = [(dy, dc) for dy in range(NY) for dc in range(NC)]
     core_peer = dev(x, zl, y, zh, 1 - c)
 
@@ -74,6 +75,7 @@
     peers = [dev(x, zl, rot(y, dy, 4), zh, rot(c, dc, 2)) for dy, dc in near[1:]]
     peers += [dev(x, zl, rot(y, dy, 4), 1 - zh, rot(c, dc, 2)) for dy, dc in near]
     peers += [dev(rot(x, d, 4), zl, y, zh, c) for d in range(1, 4)]
+    peers += [dev(rot(x, d, 4), zl, y, zh, 1 - c) for d in range(1, 4)]
     peers += [dev(x, rot(zl, d, 4), y, zh, c) for d in range(1, 4)]
     peers += [dev(x, rot(zl, d, 4), y, 1 - zh, c) for d in range(1, 4)]
     peers += [l_from]
@@ -160,25 +162,39 @@
             preferred_element_type=F32,
         )
         tt[ch, n] = part.reshape(32, 8, 128)
+        if n == D:
+            tb[ch] = part.astype(BF16).reshape(8, 32, 128)
+            for k, (dx, dc) in enumerate(others):
+                to_x, to_c = rot(x, dx, 4), rot(c, dc, 2)
+                send(
+                    tb.at[ch, to_c * 4 + to_x], xb.at[ch, k], x_s.at[ch, n], x_r.at[ch, n],
+                    dev(to_x, zl, y, zh, to_c),
+                )
+            return
         send(
-            tt.at[ch, n, pl.ds((1 - c) * 16, 16)], c1.at[ch, n],
-            core_s.at[ch, n], core_r.at[ch, n], core_peer,
+            tt.at[ch, n, pl.ds((1 - c) * 16, 16)], c1.at[ch], core_s.at[ch], core_r.at[ch], core_peer,
         )
 
     def step_b(ch, n):
-        wait(c1.at[ch, n], core_r.at[ch, n])
-        total = tt[ch, n, pl.ds(c * 16, 16)] + c1[ch, n]
-        uu[ch, n] = total.reshape(4, 4, 8, 128)
+        wait(c1.at[ch], core_r.at[ch])
+        total = tt[ch, n, pl.ds(c * 16, 16)] + c1[ch]
+        uu[ch] = total.reshape(4, 4, 8, 128)
         for d in (2, 1, 3):
             to = rot(x, d, 4)
             send(
-                uu.at[ch, n, to], x1.at[ch, n, d - 1], x_s.at[ch, n], x_r.at[ch, n],
+                uu.at[ch, to], x1.at[ch, d - 1], x_s.at[ch, n], x_r.at[ch, n],
                 dev(to, zl, y, zh, c),
             )
 
     def step_c(ch, n):
-        wait(x1.at[ch, n], x_r.at[ch, n])
-        ww[ch, n] = (uu[ch, n, x] + x1[ch, n, 0]) + (x1[ch, n, 1] + x1[ch, n, 2])
+        if n == D:
+            wait(xb.at[ch], x_r.at[ch, n])
+            part = [xb[ch, k].astype(F32) for k in range(7)]
+            total = ((part[0] + part[1]) + (part[2] + part[3])) + ((part[4] + part[5]) + part[6])
+            ww[ch, n] = tt[ch, n, pl.ds(c * 16 + x * 4, 4)] + total.reshape(4, 8, 128)
+        else:
+            wait(x1.at[ch], x_r.at[ch, n])
+            ww[ch, n] = (uu[ch, x] + x1[ch, 0]) + (x1[ch, 1] + x1[ch, 2])
         for d in range(4):
             to = rot(zl, d, 4)
             send(
@@ -303,34 +319,18 @@
         put(ch, 0, dq)
         give(ch, pl.ds(0, 2), 1)
 
-    def unpack(a, ref, hbm):
-        for tile in range(6):
-            pair = []
-            for head in (2 * tile, 2 * tile + 1):
-                yy, ch = head // CH, head % CH
-                pair.append(orr[ch, pl.ds(yy * 2, 2), a].reshape(4, 16, 128))
-            first, second = swap_halves(*pair)
-            lanes = pl.ds(tile * 128, 128)
-            for n in range(4):
-                ref[2 * n, :, lanes] = first[n]
-                ref[2 * n + 1, :, lanes] = second[n]
-        pltpu.make_async_copy(ref, hbm, store_s.at[a]).start()
-
     def step_hp(ch):
         for n in range(CH):
             wait(orr.at[n, :, pl.ds(2, 1)], out_r.at[n, 0])
-        unpack(2, dv_ref, dv_hbm)
 
     def step_hd(ch):
         for n in range(CH):
             wait(orr.at[n, :, pl.ds(0, 2)], out_r.at[n, 1])
-        unpack(1, dk_ref, dk_hbm)
-        unpack(0, dq_ref, dq_hbm)
 
     steps = {
         "I": step_i, "J": step_j, "K": step_k, "L": step_l,
         "As": lambda ch: step_a(ch, S), "Ad": lambda ch: step_a(ch, D),
-        "Bs": lambda ch: step_b(ch, S), "Bd": lambda ch: step_b(ch, D),
+        "Bs": lambda ch: step_b(ch, S),
         "Cs": lambda ch: step_c(ch, S), "Cd": lambda ch: step_c(ch, D),
         "Ds": step_p, "Dp": step_dp, "Ep": step_ep, "Fp": step_fp, "Gp": step_gp, "Hp": step_hp,
         "Dd": step_dd, "Ed": step_ed, "Fd": step_fd, "Gd": step_gd, "Hd": step_hd,
@@ -348,9 +348,10 @@
             wait(st.at[ch, :, pl.ds(a, 1)], in_s.at[ch, n])
         for a, n in ((Q, 1), (G, 3)):
             wait(st.at[ch, pl.ds(0, 7), pl.ds(a, 2)], in_s.at[ch, n])
+        wait(c1.at[ch], core_s.at[ch])
+        wait(x1.at[ch], x_s.at[ch, S])
+        wait(xb.at[ch], x_s.at[ch, D])
         for n in range(2):
-            wait(c1.at[ch, n], core_s.at[ch, n])
-            wait(x1.at[ch, n], x_s.at[ch, n])
             wait(z1.at[ch, n], z_s.at[ch, n])
         for n in range(3):
             wait(agd.at[ch, c, x, zl], gd_s.at[ch, 0, n])
@@ -358,29 +359,51 @@
         wait(agd.at[ch, c], gd_s.at[ch, 2, 0])
         wait(oo.at[ch, pl.ds(0, 7), pl.ds(2, 1)], out_s.at[ch, 0])
         wait(oo.at[ch, pl.ds(0, 7), pl.ds(0, 2)], out_s.at[ch, 1])
-    for a, (ref, hbm) in enumerate(((dq_ref, dq_hbm), (dk_ref, dk_hbm), (dv_ref, dv_hbm))):
-        pltpu.make_async_copy(ref, hbm, store_s.at[a]).wait()
+
+
+def unpack(packed, dq_hbm, dk_hbm, dv_hbm, got, done, load_s, store_s):
+    out = (dq_hbm, dk_hbm, dv_hbm)
+    loads = [pltpu.make_async_copy(packed.at[:, :, a], got.at[a], load_s.at[a]) for a in range(3)]
+    stores = [pltpu.make_async_copy(done.at[a], out[a], store_s.at[a]) for a in range(3)]
+    for load in loads:
+        load.start()
+    for a in range(3):
+        loads[a].wait()
+        for tile in range(6):
+            pair = []
+            for head in (2 * tile, 2 * tile + 1):
+                yy, ch = head // CH, head % CH
+                pair.append(got[a, ch, pl.ds(yy * 2, 2)].reshape(4, 16, 128))
+            first, second = swap_halves(*pair)
+            lanes = pl.ds(tile * 128, 128)
+            for n in range(4):
+                done[a, 2 * n, :, lanes] = first[n]
+                done[a, 2 * n + 1, :, lanes] = second[n]
+        stores[a].start()
+    for store in stores:
+        store.wait()
 
 
 def body(query_proj, key_proj, value_proj, grad_output, log_totals):
     dma = pltpu.SemaphoreType.DMA
     anywhere = pl.BlockSpec(memory_space=pl.ANY)
-    return pl.pallas_call(
+    packed = pl.pallas_call(
         kernel,
-        out_shape=[jax.ShapeDtypeStruct(query_proj.shape, BF16)] * 3,
+        out_shape=jax.ShapeDtypeStruct((CH, 8, 3, 2, 16, 128), BF16),
         in_specs=[anywhere] * 5,
-        out_specs=[anywhere] * 3,
+        out_specs=anywhere,
         scratch_shapes=[
             *[pltpu.VMEM(query_proj.shape, BF16)] * 4,
             pltpu.VMEM(log_totals.shape, F32),
-            *[pltpu.VMEM(query_proj.shape, BF16)] * 3,
-            dma((5,)), dma((3,)),
+            dma((5,)),
             pltpu.VMEM((CH, 8, 4, 2, 16, 128), BF16),
             pltpu.VMEM((CH, 2, 8, 4, 2, 16, 128), BF16),
             pltpu.VMEM((CH, 2, 32, 8, 128), F32),
-            pltpu.VMEM((CH, 2, 16, 8, 128), F32),
-            pltpu.VMEM((CH, 2, 4, 4, 8, 128), F32),
-            pltpu.VMEM((CH, 2, 3, 4, 8, 128), F32),
+            pltpu.VMEM((CH, 8, 32, 128), BF16),
+            pltpu.VMEM((CH, 7, 32, 128), BF16),
+            pltpu.VMEM((CH, 16, 8, 128), F32),
+            pltpu.VMEM((CH, 4, 4, 8, 128), F32),
+            pltpu.VMEM((CH, 3, 4, 8, 128), F32),
             pltpu.VMEM((CH, 2, 4, 8, 128), F32),
             pltpu.VMEM((CH, 2, 7, 8, 128), F32),
             pltpu.VMEM((CH, 2, 8, 128), F32),
@@ -389,11 +412,10 @@
             pltpu.VMEM((CH, 2, 4, 4, 16, 128), BF16),
             pltpu.VMEM((CH, 16, 128), BF16),
             pltpu.VMEM((CH, 8, 3, 2, 16, 128), BF16),
-            pltpu.VMEM((CH, 8, 3, 2, 16, 128), BF16),
             pltpu.VMEM((CH, 8, 128), F32),
             pltpu.VMEM((CH, 8, 128), F32),
             dma((CH, 5)), dma((CH, 5)),
-            dma((CH, 2)), dma((CH, 2)),
+            dma((CH,)), dma((CH,)),
             dma((CH, 2)), dma((CH, 2)),
             dma((CH, 2)), dma((CH, 2)),
             dma((3, 3)), dma((3, 3)),
@@ -406,6 +428,19 @@
         ),
         name="tied_row_backward",
     )(query_proj, key_proj, value_proj, grad_output, log_totals)
+    return pl.pallas_call(
+        unpack,
+        out_shape=[jax.ShapeDtypeStruct(query_proj.shape, BF16)] * 3,
+        in_specs=[anywhere],
+        out_specs=[anywhere] * 3,
+        scratch_shapes=[
+            pltpu.VMEM((3, CH, 8, 2, 16, 128), BF16),
+            pltpu.VMEM((3, *query_proj.shape), BF16),
+            dma((3,)), dma((3,)),
+        ],
+        compiler_params=pltpu.CompilerParams(vmem_limit_bytes=60 * 2**20),
+        name="unpack_gradients",
+    )(packed)
 
 
 def solution(mesh):

time: 68.9 us -> 65 us (0.943)
  local copies, waits for them, and re-layouts: 3.33 us -> 0 us
    unnamed x7 -> x0, local copies, waits for them, and re-layouts: 3.33 us -> none
    pallas_call x1 -> x2, Pallas kernels: 64.7 us -> 64.2 us  [the longest x1 62.2 us: body(): pl.pallas_call(kernel, out_shape=jax.ShapeDtypeStruct((CH, 8, 3, 2, 16, 1...]
where the time goes in v3:
time: 65 us; the launch traced here: 64.8 us
  Pallas kernels  64.2 us (99%)
    pallas_call x1, Pallas kernels, body(): pl.pallas_call(kernel, out_shape=jax.ShapeDtypeStruct((CH, 8, 3, 2, 16, 1...  62.2 us
    pallas_call x1, Pallas kernels, body(): pl.pallas_call(unpack, out_shape=[jax.ShapeDtypeStruct(query_proj.shape,...  2.02 us

profile of v3, /device:TPU:1, one launch (start us, length us, event | category | flops | bytes accessed | tf_op | source)
XLA Modules:
  0.0 64.8 jit_solution(5502882866206089051)
XLA Ops:
  0.6 62.2 %tied_row_backward.1.packed = bf16[3,8,3,2,16,128]{5,4,3,2,1,0:T(8,128)(2,1)} custom-call(bf16[8,16,768]{2,1,0:T(8,128)(2,1)} %q_hbm.1, bf16[8,16,768]{2,1,0:T(8,128)(2,1)} %k_hbm.1, bf16[8,16,768]{2,1,0:T(8,128)(2,1)} %v_hbm.1, bf16[8,16,768]{2,1,0:T(8,128)(2,1)} %g_hbm.1, f32[12,16]{1,0:T(8,128)} %l_hbm.1), custom_call_target="tpu_custom_call" | custom-call | tf_op jit(solution)/shard_map/tied_row_backward/pallas_call | solution.py:390
  62.8 2.0 %unpack_gradients.1 = (bf16[8,16,768]{2,1,0:T(8,128)(2,1)}, bf16[8,16,768]{2,1,0:T(8,128)(2,1)}, bf16[8,16,768]{2,1,0:T(8,128)(2,1)}) custom-call(bf16[3,8,3,2,16,128]{5,4,3,2,1,0:T(8,128)(2,1)} %tied_row_backward.1.packed), custom_call_target="tpu_custom_call" | custom-call | tf_op jit(solution)/shard_map/unpack_gradients/pallas_call | solution.py:431

commit v4 on v3

--- a/solution.py
+++ b/solution.py
@@ -14,8 +14,8 @@
 
 ORDER = (
     "I0", "L0", "I1", "I2", "J0", "J1", "J2", "As0", "Bs0", "As1", "Bs1", "As2", "Bs2", "Cs0",
-    "Cs1", "Cs2", "K0", "K1", "Ad0", "Ad1", "Cd0", "Ad2", "Cd1", "Cd2", "Ds0", "Ds1", "Ds2", "Dp0",
-    "Dd0", "Dd1", "Dd2", "K2", "Ep0", "Ed0", "Ed1", "Ed2", "Fp0", "Fd0", "Fd1", "Fd2", "Gp0", "Gp1",
+    "Cs1", "Cs2", "K0", "K1", "Ad0", "Ad1", "Cd0", "Ad2", "Cd1", "Cd2", "K2", "Ds0", "Ds1", "Ds2",
+    "Dp0", "Dd0", "Dd1", "Dd2", "Ep0", "Ed0", "Ed1", "Ed2", "Fp0", "Fd0", "Fd1", "Fd2", "Gp0", "Gp1",
     "Gp2", "Gd0", "Gd1", "Gd2", "Hp0", "Hd0",
 )
 

time: 65 us -> 66.6 us (1.025)
  Pallas kernels: 64.2 us -> 65.9 us
    pallas_call x1, Pallas kernels: 62.2 us -> 63.9 us  [body(): pl.pallas_call(kernel, out_shape=jax.ShapeDtypeStruct((CH, 8, 3, 2, 16, 1...]
where the time goes in v4:
time: 66.6 us; the launch traced here: 66.5 us
  Pallas kernels  65.9 us (99%)
    pallas_call x1, Pallas kernels, body(): pl.pallas_call(kernel, out_shape=jax.ShapeDtypeStruct((CH, 8, 3, 2, 16, 1...  63.9 us
    pallas_call x1, Pallas kernels, body(): pl.pallas_call(unpack, out_shape=[jax.ShapeDtypeStruct(query_proj.shape,...  2.02 us

profile of v4, /device:TPU:1, one launch (start us, length us, event | category | flops | bytes accessed | tf_op | source)
XLA Modules:
  0.0 66.5 jit_solution(17488668000921225305)
XLA Ops:
  0.6 63.9 %tied_row_backward.1.packed = bf16[3,8,3,2,16,128]{5,4,3,2,1,0:T(8,128)(2,1)} custom-call(bf16[8,16,768]{2,1,0:T(8,128)(2,1)} %q_hbm.1, bf16[8,16,768]{2,1,0:T(8,128)(2,1)} %k_hbm.1, bf16[8,16,768]{2,1,0:T(8,128)(2,1)} %v_hbm.1, bf16[8,16,768]{2,1,0:T(8,128)(2,1)} %g_hbm.1, f32[12,16]{1,0:T(8,128)} %l_hbm.1), custom_call_target="tpu_custom_call" | custom-call | tf_op jit(solution)/shard_map/tied_row_backward/pallas_call | solution.py:390
  64.5 2.0 %unpack_gradients.1 = (bf16[8,16,768]{2,1,0:T(8,128)(2,1)}, bf16[8,16,768]{2,1,0:T(8,128)(2,1)}, bf16[8,16,768]{2,1,0:T(8,128)(2,1)}) custom-call(bf16[3,8,3,2,16,128]{5,4,3,2,1,0:T(8,128)(2,1)} %tied_row_backward.1.packed), custom_call_target="tpu_custom_call" | custom-call | tf_op jit(solution)/shard_map/unpack_gradients/pallas_call | solution.py:431
